TPU v7x, 32 devices: a whole 2x2x4 slice. The times are simulated.
32 devices in a mesh: expert: 8 (over z, y), etp: 4 (over x, core).
Axes of the slice: x: 2, y: 2, z: 4, core: 2. Of those that a mesh axis runs over, the one named last changes fastest.
Arguments:
- tokens: bfloat16 [1024, 4096], P('expert', 'etp'), may hold values from -6 to 6
- expert_ids: int32 [1024, 8], P('expert'), may hold values from 0 to 15, all different within a row; in each aligned block of 128 rows (0 to 127, 128 to 255, ...) at most 96 rows name the same one
- gate_probs: float32 [1024, 8], P('expert'), may hold values from 0.1 to 0.5
- w_gate: bfloat16 [16, 1536, 4096], P('expert', 'etp'), may hold values from -0.09375 to 0.09375
- w_up: bfloat16 [16, 1536, 4096], P('expert', 'etp'), may hold values from -0.09375 to 0.09375
- w_down: bfloat16 [16, 1536, 4096], P('expert', None, 'etp'), may hold values from -0.15625 to 0.15625
Outputs:
- moe_out: bfloat16 [1024, 4096], P('expert', 'etp')
Inputs may be any that keep to these rules, and one draw needn't show every extreme that they name: `expert_ids`: within each aligned block of 128 token rows (the rows of one index of expert), no expert is named by more than 96 rows, a bound that some block reaches; the 8 experts of a row differ.
All inputs are finite; a program needn't handle non-finite values.
Results may differ from a plain program's by a relative error of at most 0.0058.
Values may be sent and summed in bfloat16 or wider, within the bound.
A program may use at most 128 MiB of HBM per device.

v0:
```python
import jax
import jax.numpy as jnp
from jax import lax
from jax.sharding import PartitionSpec as P


def on_device(tokens, expert_ids, gate_probs, w_gate, w_up, w_down):
    tok_rows = tokens.shape[0]
    top_count = expert_ids.shape[1]
    owners = lax.axis_size("expert")
    local_experts = w_gate.shape[0]
    expert_count = owners * local_experts
    capacity = 3 * tok_rows * top_count // (2 * expert_count)
    pairs = expert_ids.reshape(-1)
    onehot = (pairs[:, None] == jnp.arange(expert_count, dtype=jnp.int32)[None, :]).astype(
        jnp.int32
    )
    position = jnp.sum(jnp.cumsum(onehot, axis=0) * onehot, axis=1) - 1
    slot_index = pairs * capacity + position
    token_of = jnp.arange(pairs.shape[0], dtype=jnp.int32) // top_count
    source_row = (
        jnp.full((expert_count * capacity,), tok_rows, jnp.int32).at[slot_index].set(token_of)
    )
    padded = jnp.concatenate([tokens, jnp.zeros((1, tokens.shape[1]), tokens.dtype)], axis=0)
    outgoing = padded[source_row].reshape(owners, local_experts, capacity, tokens.shape[1])
    full_rows = lax.all_gather(
        lax.all_to_all(outgoing, "expert", split_axis=0, concat_axis=0, tiled=True),
        "etp",
        axis=3,
        tiled=True,
    )
    gate = jnp.einsum("sjcd,jfd->sjcf", full_rows, w_gate, preferred_element_type=jnp.float32)
    upper = jnp.einsum("sjcd,jfd->sjcf", full_rows, w_up, preferred_element_type=jnp.float32)
    hidden = (jax.nn.silu(gate) * upper).astype(jnp.bfloat16)
    hidden_all = lax.all_gather(hidden, "etp", axis=3, tiled=True)
    result = jnp.einsum("sjcf,jfd->sjcd", hidden_all, w_down, preferred_element_type=jnp.float32)
    returned = lax.all_to_all(
        result.astype(jnp.bfloat16), "expert", split_axis=0, concat_axis=0, tiled=True
    )
    results = returned.reshape(expert_count * capacity, returned.shape[3])
    picked = results[slot_index].astype(jnp.float32) * gate_probs.reshape(-1)[:, None]
    mixed = jnp.sum(picked.reshape(tok_rows, top_count, results.shape[1]), axis=1)
    return mixed.astype(jnp.bfloat16)


def solution(mesh):
    return jax.shard_map(
        on_device,
        mesh=mesh,
        in_specs=(
            P("expert", "etp"),
            P("expert", None),
            P("expert", None),
            P("expert", "etp", None),
            P("expert", "etp", None),
            P("expert", None, "etp"),
        ),
        out_specs=P("expert", "etp"),
        check_vma=False,
    )
```

profile of v0, /device:TPU:0, one launch (start us, length us, event | category | flops | bytes accessed | tf_op | source)
XLA Modules:
  0.0 347.4 jit_solution(4548147534294592357)
XLA Ops:
  6.5 0.0 all-gather.3.cloned.1.call-start
  6.5 0.8 copy.19
  7.3 0.1 eq.29
  7.4 0.1 eq.25
  7.5 0.7 broadcast_multiply_fusion
  8.2 4.5 %reduce-window.6 = s32[16,8,128]{2,1,0:T(8,128)S(1)} reduce-window(s32[16,8,128]{2,1,0:T(8,128)S(1)} %fusion.17, s32[]{:T(128)} %constant.33.clone.1), window={size=1x1x128 pad=0_0x0_0x127_0}, to_apply=%region_0.0 | reduce-window | flops 2080768 | bytes 131076 | tf_op jit(solution)/shard_map/reduce-window
  12.7 0.1 slice.12
  12.8 0.1 copy.21
  13.0 0.1 copy.22
  13.1 0.1 broadcast_add_fusion
  13.2 0.1 copy.18
  13.3 0.1 mul.37
  13.4 4.3 %scatter_custom_fusion = s32[1536]{0:T(1024)S(1)} fusion(s32[1024]{0:T(1024)S(1)} %bitcast.66, s32[1024]{0:T(1024)S(1)} %add_select_fusion, s32[]{:T(128)} %constant.31.clone.1), kind=kCustom, calls=%fused_computation.35 | custom fusion | bytes 6148 | tf_op jit(solution)/shard_map/scatter | solution.py:22
  17.8 1.0 concatenate.3
  18.7 5.1 %gather_fusion = bf16[1536,1024]{1,0:T(8,128)(2,1)S(1)} fusion(bf16[129,1024]{1,0:T(8,128)(2,1)S(1)} %concatenate.3, s32[2048]{0:T(1024)S(1)} %pad_clamp_fusion), kind=kCustom, calls=%fused_computation | custom fusion | bytes 6297600 | tf_op jit(solution)/shard_map/gather | solution.py:25
  23.8 77.8 %all_to_all.10 = bf16[8,2,96,1024]{3,2,1,0:T(8,128)(2,1)S(1)} all-to-all(bf16[8,2,96,1024]{3,2,1,0:T(8,128)(2,1)S(1)} %bitcast.63), channel_id=1, replica_groups=mesh['expert'=8,'etp'=4] {'expert'}, dimensions={0} | all-to-all | bytes 6291456 | tf_op jit(solution)/shard_map/all_to_all | solution.py:27
  101.6 2.1 copy.23
  103.7 0.0 all-gather.3.cloned.1.call-update
  103.7 0.0 all-gather.5.cloned.1.call-start
  103.8 81.2 %all-gather.3.cloned.1.call-done = bf16[8,2,96,4096]{3,2,0,1:T(8,128)(2,1)} async-done(((bf16[8,2,96,1024]{3,2,0,1:T(8,128)(2,1)}), bf16[8,2,96,4096]{3,2,0,1:T(8,128)(2,1)}) %all-gather.3.cloned.1.call-update) | async-done | bytes 12582928 | tf_op jit(solution)/shard_map/all_gather | solution.py:26
  185.0 0.0 copy-start.1
  185.0 11.8 %fusion.2 = f32[2,8,96,384]{3,2,1,0:T(8,128)S(1)} fusion(bf16[8,2,96,4096]{3,2,0,1:T(8,128)(2,1)} %all-gather.3.cloned.1.call-done, bf16[2,384,4096]{2,1,0:T(8,128)(2,1)} %param.10), kind=kOutput, calls=%fused_computation.5 | convolution fusion | flops 4831838208 | bytes 21233664 | tf_op jit(solution)/shard_map/sjcd,jfd->sjcf/dot_general | solution.py:33
  196.8 0.0 copy-done.1
  196.8 9.8 %fusion.7 = bf16[8,2,96,384]{3,2,0,1:T(8,128)(2,1)} fusion(f32[2,8,96,384]{3,2,1,0:T(8,128)S(1)} %fusion.2, bf16[8,2,96,4096]{3,2,0,1:T(8,128)(2,1)S(1)} %copy-done.1, bf16[2,384,4096]{2,1,0:T(8,128)(2,1)} %param.9), kind=kOutput, calls=%fused_computation.13 | convolution fusion | flops 4835377152 | bytes 22413312 | tf_op jit(solution)/shard_map/sjcd,jfd->sjcf/dot_general | solution.py:32
  206.6 0.0 all-gather.5.cloned.1.call-update
  206.7 37.6 %all-gather.5.cloned.1.call-done = bf16[8,2,96,1536]{3,2,0,1:T(8,128)(2,1)} async-done(((bf16[8,2,96,384]{3,2,0,1:T(8,128)(2,1)}), bf16[8,2,96,1536]{3,2,0,1:T(8,128)(2,1)}) %all-gather.5.cloned.1.call-update) | async-done | bytes 4718608 | tf_op jit(solution)/shard_map/all_gather | solution.py:35
  244.2 8.6 %convert_bitcast_fusion = bf16[8,2,96,1024]{3,2,0,1:T(8,128)(2,1)S(1)} fusion(bf16[8,2,96,1536]{3,2,0,1:T(8,128)(2,1)} %all-gather.5.cloned.1.call-done, bf16[2,1536,1024]{2,1,0:T(8,128)(2,1)} %param.11), kind=kOutput, calls=%fused_computation.11 | convolution fusion | flops 4833411072 | bytes 14155776 | tf_op jit(solution)/shard_map/sjcf,jfd->sjcd/dot_general | solution.py:36
  252.8 2.0 copy.24
  254.7 0.0 copy-start
  254.7 5.6 %all-to-all-start.1 = ((bf16[8,2,96,1024]{3,2,1,0:T(8,128)(2,1)}), bf16[8,2,96,1024]{3,2,1,0:T(8,128)(2,1)S(1)}, u32[]{:S(2)}, u32[]{:S(2)}) async-start(bf16[8,2,96,1024]{3,2,1,0:T(8,128)(2,1)} %copy.24), calls=%async_computation.1 | async-start | bytes 6291456 | tf_op jit(solution)/shard_map/all_to_all | solution.py:37
  260.4 0.0 copy-done
  260.4 0.1 copy.25
  260.5 71.0 %all-to-all-done.1 = bf16[8,2,96,1024]{3,2,1,0:T(8,128)(2,1)S(1)} async-done(((bf16[8,2,96,1024]{3,2,1,0:T(8,128)(2,1)}), bf16[8,2,96,1024]{3,2,1,0:T(8,128)(2,1)S(1)}, u32[]{:S(2)}, u32[]{:S(2)}) %all-to-all-start.1) | async-done | bytes 3145760 | tf_op jit(solution)/shard_map/all_to_all | solution.py:37
  331.5 5.4 %gather_fusion.1 = bf16[1024,1024]{1,0:T(8,128)(2,1)} fusion(bf16[1536,1024]{1,0:T(8,128)(2,1)S(1)} %bitcast.62, s32[1024]{0:T(1024)S(1)} %broadcast_clamp_fusion), kind=kCustom, calls=%fused_computation.1 | custom fusion | bytes 4198400 | tf_op jit(solution)/shard_map/gather | solution.py:41
  336.9 3.7 %fusion.6 = bf16[128,1024]{1,0:T(8,128)(2,1)} fusion(bf16[1024,1024]{1,0:T(8,128)(2,1)} %gather_fusion.1, f32[128,8]{1,0:T(8,128)S(1)} %copy.25), kind=kLoop, calls=%fused_computation.10 | loop fusion | flops 3014656 | bytes 2363392 | tf_op jit(solution)/shard_map/reduce_sum | solution.py:42
  (10 shorter events, 0.1 us)
Async XLA Ops:
  6.5 178.4 %all-gather.3.cloned.1.call-start = ((), (), s32[]{:S(2)}) async-start(), calls=%async_computation.2 | async-start | bytes 15728640 | tf_op jit(solution)/shard_map/all_gather | solution.py:26
  103.7 140.5 %all-gather.5.cloned.1.call-start = ((), (), s32[]{:S(2)}) async-start(), calls=%async_computation.3 | async-start | bytes 5898240 | tf_op jit(solution)/shard_map/all_gather | solution.py:35
  185.0 11.8 %copy-start.1 = (bf16[8,2,96,4096]{3,2,0,1:T(8,128)(2,1)S(1)}, bf16[8,2,96,4096]{3,2,0,1:T(8,128)(2,1)}, u32[]{:S(2)}) copy-start(bf16[8,2,96,4096]{3,2,0,1:T(8,128)(2,1)} %all-gather.3.cloned.1.call-done) | copy-start | bytes 37748740
  254.7 5.7 %copy-start = (f32[128,8]{0,1:T(8,128)S(1)}, f32[128,8]{0,1:T(8,128)}, u32[]{:S(2)}) copy-start(f32[128,8]{0,1:T(8,128)} %param.8) | copy-start | bytes 12292
  254.7 76.8 %all-to-all-start.1 = ((bf16[8,2,96,1024]{3,2,1,0:T(8,128)(2,1)}), bf16[8,2,96,1024]{3,2,1,0:T(8,128)(2,1)S(1)}, u32[]{:S(2)}, u32[]{:S(2)}) async-start(bf16[8,2,96,1024]{3,2,1,0:T(8,128)(2,1)} %copy.24), calls=%async_computation.1 | async-start | bytes 6291456 | tf_op jit(solution)/shard_map/all_to_all | solution.py:37
Sparse Core Ops, SparseCore 0:
  103.8 81.0 all-gather.2
  206.8 37.3 all-gather.4
where the time goes:
time: 348 us; the launch traced here: 347 us
  waiting for transfers between devices  190 us (55%)
  blocking collectives  77.8 us (22%)
  matrix products  30.2 us (9%)
  local copies, waits for them, and re-layouts  21.3 us (6%)
  between operations  13.5 us (4%)
  other arithmetic  9.05 us (3%)
  starting transfers between devices  5.69 us (2%)
    all_gather x1, waiting for transfers between devices, on_device(): lax.all_gather(lax.all_to_all(outgoing, 'expert', split_axis=0, concat_ax...  81.2 us
    all_to_all x1, blocking collectives, on_device(): lax.all_to_all(outgoing, 'expert', split_axis=0, concat_axis=0, tiled=True)  77.8 us
    all_to_all x1, waiting for transfers between devices, on_device(): lax.all_to_all(result.astype(jnp.bfloat16), 'expert', split_axis=0, conca...  71 us
    all_gather x1, waiting for transfers between devices, on_device(): hidden_all = lax.all_gather(hidden, 'etp', axis=3, tiled=True)  37.6 us
    dot_general x1, matrix products, on_device(): jnp.einsum('sjcd,jfd->sjcf', full_rows, w_up, preferred_element_type=jnp....  11.8 us
    dot_general x1, matrix products, on_device(): jnp.einsum('sjcd,jfd->sjcf', full_rows, w_gate, preferred_element_type=jn...  9.83 us
    dot_general x1, matrix products, on_device(): jnp.einsum('sjcf,jfd->sjcd', hidden_all, w_down, preferred_element_type=j...  8.55 us
  transfers between devices with their start and end apart: 3, of which 3 were waited for; matrix products, arithmetic and copies ran while one was open for 0% of the time, Pallas kernels for 0%

commit v1 on v0

--- a/solution.py
+++ b/solution.py
@@ -1,10 +1,17 @@
+import functools
 import jax
 import jax.numpy as jnp
 from jax import lax
+from jax.experimental import pallas as pl
+from jax.experimental.pallas import tpu as pltpu
 from jax.sharding import PartitionSpec as P
 
-
-def on_device(tokens, expert_ids, gate_probs, w_gate, w_up, w_down):
+MESH = pl.DeviceIdType.MESH
+VMEM_BUDGET = 60 * 2**20
+PAIR = 2
+
+
+def routed(tokens, expert_ids, gate_probs, w_gate, w_up, w_down):
     tok_rows = tokens.shape[0]
     top_count = expert_ids.shape[1]
     owners = lax.axis_size("expert")
@@ -43,9 +50,257 @@
     return mixed.astype(jnp.bfloat16)
 
 
+def fused_kernel(
+    owners, splits,
+    own_ref, ids_ref, probs_ref, wg_hbm, wu_hbm, wd_hbm,
+    out_ref,
+    tok, wg, wu, wd, hid, share, acc, ysend, yrecv, zsend, zrecv,
+    w_sem, send_sem, tok_sem, share_sem, hid_sem, y_sem, z_sem,
+):
+    rows, cols = own_ref.shape
+    local_experts, units = wg_hbm.shape[0], wg_hbm.shape[1]
+    ny = PAIR
+    nz = owners // ny
+    me, part = lax.axis_index("expert"), lax.axis_index("etp")
+    z, y = me // ny, me % ny
+    other_y = 1 - y
+    x, core = part // PAIR, part % PAIR
+    part_x = (1 - x) * PAIR + core
+    part_sib = x * PAIR + (1 - core)
+    part_sib_x = (1 - x) * PAIR + (1 - core)
+    dev_x, dev_sib, dev_y = (me, part_x), (me, part_sib), (z * ny + other_y, part)
+
+    loads = [
+        pltpu.make_async_copy(src, dst, w_sem.at[i])
+        for i, (src, dst) in enumerate(((wg_hbm, wg), (wu_hbm, wu), (wd_hbm, wd)))
+    ]
+    for load in loads:
+        load.start()
+
+    barrier = pltpu.get_barrier_semaphore()
+    peers = [(lax.rem(me + k, owners), part) for k in range(1, owners)] + [dev_x, dev_sib]
+    for peer in peers:
+        pl.semaphore_signal(barrier, inc=1, device_id=peer, device_id_type=MESH)
+
+    ids, probs = ids_ref[...], probs_ref[...]
+    for e in range(owners * local_experts):
+        share[me, e : e + 1, :] = jnp.sum(
+            jnp.where(ids == e, probs, 0.0), axis=0, keepdims=True
+        )
+
+    pl.semaphore_wait(barrier, len(peers))
+
+    sends = []
+
+    def send(src, dst, arrived, device):
+        copy = pltpu.make_async_remote_copy(
+            src_ref=src, dst_ref=dst, send_sem=send_sem.at[len(sends)], recv_sem=arrived,
+            device_id=device, device_id_type=MESH,
+        )
+        copy.start()
+        sends.append(copy)
+
+    def await_arrival(dst, arrived):
+        pltpu.make_async_remote_copy(
+            src_ref=dst, dst_ref=dst, send_sem=send_sem.at[0], recv_sem=arrived,
+            device_id=dev_sib, device_id_type=MESH,
+        ).wait_recv()
+
+    def tok_at(s, t):
+        return tok.at[
+            pl.ds(pl.multiple_of(s * rows, rows), rows), pl.ds(pl.multiple_of(t * cols, cols), cols)
+        ]
+
+    def send_tok(s, t, device, src=None):
+        block = tok_at(s, t)
+        send(block if src is None else src, block, tok_sem.at[s, t], device)
+
+    def await_tok(s, t):
+        await_arrival(tok_at(s, t), tok_sem.at[s, t])
+
+    def z_of(k):
+        return lax.rem(z - k + nz, nz)
+
+    z_peers = [(lax.rem(z + k, nz) * ny + y, part) for k in range(1, nz)]
+    send_tok(me, part, dev_x, own_ref)
+    send_tok(me, part, dev_y, own_ref)
+    for peer in z_peers:
+        send_tok(me, part, peer, own_ref)
+    send_tok(me, part, dev_sib, own_ref)
+    for peer in peers[: owners - 1]:
+        send(share.at[me], share.at[me], share_sem.at[me], peer)
+    tok[
+        pl.ds(pl.multiple_of(me * rows, rows), rows), pl.ds(pl.multiple_of(part * cols, cols), cols)
+    ] = own_ref[...]
+    await_tok(me, part_x)
+    send_tok(me, part_x, dev_y)
+    for peer in z_peers:
+        send_tok(me, part_x, peer)
+    send_tok(me, part_x, dev_sib)
+
+    def forward_z(k):
+        s = z_of(k) * ny + y
+        for t in (part, part_x):
+            await_tok(s, t)
+            send_tok(s, t, dev_y)
+            send_tok(s, t, dev_sib)
+
+    def finish_tokens(k):
+        mine, other = z_of(k) * ny + y, z_of(k) * ny + other_y
+        for t in (part, part_x):
+            await_tok(other, t)
+            send_tok(other, t, dev_sib)
+        for s in (mine, other):
+            for t in (part_sib, part_sib_x):
+                await_tok(s, t)
+
+    group = ny * rows
+
+    def group_rows(k):
+        return pl.ds(pl.multiple_of(z_of(k) * group, group), group)
+
+    def hid_at(k, t):
+        return hid.at[:, group_rows(k), pl.ds(pl.multiple_of(t * units, units), units)]
+
+    nt = (((1,), (1,)), ((), ()))
+
+    def gate_up(k):
+        for j in range(local_experts):
+            inputs = tok[group_rows(k), :]
+            gate = lax.dot_general(inputs, wg[j], nt, preferred_element_type=jnp.float32)
+            upper = lax.dot_general(inputs, wu[j], nt, preferred_element_type=jnp.float32)
+            hid[j, group_rows(k), pl.ds(pl.multiple_of(part * units, units), units)] = (
+                gate / (1.0 + jnp.exp(-gate)) * upper
+            ).astype(jnp.bfloat16)
+        for device in (dev_x, dev_sib):
+            send(hid_at(k, part), hid_at(k, part), hid_sem.at[z_of(k), part], device)
+
+    def finish_hidden(k):
+        await_arrival(hid_at(k, part_x), hid_sem.at[z_of(k), part_x])
+        send(hid_at(k, part_x), hid_at(k, part_x), hid_sem.at[z_of(k), part_x], dev_sib)
+        for t in (part_sib, part_sib_x):
+            await_arrival(hid_at(k, t), hid_sem.at[z_of(k), t])
+
+    diagonal = lax.broadcasted_iota(jnp.int32, (rows, rows), 0) == lax.broadcasted_iota(
+        jnp.int32, (rows, rows), 1
+    )
+
+    def down(k):
+        for j in range(local_experts):
+            result = jnp.dot(hid[j, group_rows(k), :], wd[j], preferred_element_type=jnp.float32)
+            for i in range(ny):
+                line = share[z_of(k) * ny + i, pl.ds(me * local_experts + j, 1), :]
+                column = jnp.sum(
+                    jnp.where(diagonal, jnp.broadcast_to(line, (rows, rows)), 0.0),
+                    axis=1, keepdims=True,
+                )
+                term = result[i * rows : (i + 1) * rows] * column
+                if j == 0:
+                    acc[k, i] = term
+                else:
+                    acc[k, i] += term
+        ysend[k] = acc[k, other_y].astype(jnp.bfloat16)
+        send(ysend.at[k], yrecv.at[k], y_sem.at[k], dev_y)
+
+    def reduce_y(k):
+        await_arrival(yrecv.at[k], y_sem.at[k])
+        total = acc[k, y] + yrecv[k].astype(jnp.float32)
+        if k == 0:
+            acc[0, y] = total
+        else:
+            zsend[k] = total.astype(jnp.bfloat16)
+            send(zsend.at[k], zrecv.at[k], z_sem.at[k], (z_of(k) * ny + y, part))
+
+    if nz > 1:
+        forward_z(1)
+    for k in range(nz):
+        finish_tokens(k)
+        if k == 0:
+            loads[0].wait()
+            loads[1].wait()
+        gate_up(k)
+        if k > 0:
+            reduce_y(k - 1)
+        if k + 2 < nz:
+            forward_z(k + 2)
+        if k == 0:
+            loads[2].wait()
+            for i in range(1, owners):
+                s = lax.rem(me + i, owners)
+                await_arrival(share.at[s], share_sem.at[s])
+        finish_hidden(k)
+        down(k)
+    reduce_y(nz - 1)
+    total = acc[0, y]
+    for k in range(1, nz):
+        await_arrival(zrecv.at[k], z_sem.at[k])
+        total = total + zrecv[k].astype(jnp.float32)
+    out_ref[...] = total.astype(jnp.bfloat16)
+    for copy in sends:
+        copy.wait_send()
+
+
+def fused(owners, splits, tokens, expert_ids, gate_probs, w_gate, w_up, w_down):
+    rows, cols = tokens.shape
+    local_experts, units, width = w_gate.shape
+    nz = owners // PAIR
+    everything = owners * rows
+    bf16, f32 = jnp.bfloat16, jnp.float32
+    vmem = pl.BlockSpec(memory_space=pltpu.VMEM)
+    hbm = pl.BlockSpec(memory_space=pl.ANY)
+    dma = pltpu.SemaphoreType.DMA
+    count = 2 * (nz + 2) + (owners - 1) + 4 * (nz - 1) + 2 * nz + 3 * nz + nz + nz
+    flops = 6 * everything * local_experts * units * width
+    return pl.pallas_call(
+        functools.partial(fused_kernel, owners, splits),
+        out_shape=jax.ShapeDtypeStruct((rows, cols), bf16),
+        in_specs=[vmem, vmem, vmem, hbm, hbm, hbm],
+        out_specs=vmem,
+        scratch_shapes=[
+            pltpu.VMEM((everything, width), bf16),
+            pltpu.VMEM(w_gate.shape, bf16),
+            pltpu.VMEM(w_up.shape, bf16),
+            pltpu.VMEM(w_down.shape, bf16),
+            pltpu.VMEM((local_experts, everything, w_down.shape[1]), bf16),
+            pltpu.VMEM((owners, owners * local_experts, rows), f32),
+            pltpu.VMEM((nz, PAIR, rows, cols), f32),
+            pltpu.VMEM((nz, rows, cols), bf16),
+            pltpu.VMEM((nz, rows, cols), bf16),
+            pltpu.VMEM((nz, rows, cols), bf16),
+            pltpu.VMEM((nz, rows, cols), bf16),
+            dma((3,)),
+            dma((count,)),
+            dma((owners, splits)),
+            dma((owners,)),
+            dma((nz, splits)),
+            dma((nz,)),
+            dma((nz,)),
+        ],
+        compiler_params=pltpu.CompilerParams(
+            collective_id=0, has_side_effects=True, vmem_limit_bytes=VMEM_BUDGET
+        ),
+        cost_estimate=pl.CostEstimate(
+            flops=flops, bytes_accessed=6 * w_gate.size, transcendentals=0
+        ),
+        name="moe",
+    )(tokens, expert_ids.T, gate_probs.T, w_gate, w_up, w_down)
+
+
+def on_device(owners, splits, tokens, expert_ids, gate_probs, w_gate, w_up, w_down):
+    rows, cols = tokens.shape
+    local_experts, units, width = w_gate.shape
+    everything = owners * rows
+    need = 2 * (everything * width + 3 * w_gate.size + local_experts * everything * units * splits)
+    need += owners * rows * cols * 8 + 6 * rows * local_experts * width
+    fits = need <= VMEM_BUDGET and rows % 128 == 0 and cols % 128 == 0 and units % 128 == 0
+    if fits and splits == PAIR * PAIR and owners % PAIR == 0:
+        return fused(owners, splits, tokens, expert_ids, gate_probs, w_gate, w_up, w_down)
+    return routed(tokens, expert_ids, gate_probs, w_gate, w_up, w_down)
+
+
 def solution(mesh):
     return jax.shard_map(
-        on_device,
+        functools.partial(on_device, mesh.shape["expert"], mesh.shape["etp"]),
         mesh=mesh,
         in_specs=(
             P("expert", "etp"),

time: 348 us -> 143 us (0.41)
  the two profiles are of different devices: /device:TPU:0 before, /device:TPU:24 now
where the time goes in v1:
time: 143 us
  Pallas kernels  141 us (99%)
  local copies, waits for them, and re-layouts  1.67 us (1%)
    pallas_call x1, Pallas kernels, fused(): pl.pallas_call(functools.partial(fused_kernel, owners, splits), out_shape...  141 us

profile of v1, /device:TPU:24, one launch (start us, length us, event | category | flops | bytes accessed | tf_op | source)
XLA Modules:
  0.0 142.6 jit_solution(7470091958293936830)
XLA Ops:
  0.0 140.9 %moe.1 = bf16[128,1024]{1,0:T(8,128)(2,1)} custom-call(bf16[128,1024]{1,0:T(8,128)(2,1)} %own_ref.1, s32[8,128]{1,0:T(8,128)} %bitcast.2, f32[8,128]{1,0:T(8,128)} %bitcast.3, bf16[2,384,4096]{2,1,0:T(8,128)(2,1)} %wg_hbm.1, bf16[2,384,4096]{2,1,0:T(8,128)(2,1)} %wu_hbm.1, bf16[2,1536,1024]{2,1,0:T(8,128)(2,1)} %wd_hbm.1), custom_call_target="tpu_custom_call" | custom-call | flops 19327352832 | bytes 18874368 | tf_op jit(solution)/shard_map/moe/pallas_call | solution.py:254
  140.9 1.7 %copy.8 = bf16[128,1024]{1,0:T(8,128)(2,1)} copy(bf16[128,1024]{1,0:T(8,128)(2,1)} %moe.1) | data formatting | bytes 524288

commit v2 on v1

--- a/solution.py
+++ b/solution.py
@@ -54,7 +54,7 @@
     owners, splits,
     own_ref, ids_ref, probs_ref, wg_hbm, wu_hbm, wd_hbm,
     out_ref,
-    tok, wg, wu, wd, hid, share, acc, ysend, yrecv, zsend, zrecv,
+    tok, turned, wg, wu, wd, hid, share, acc, ysend, yrecv, zsend, zrecv,
     w_sem, send_sem, tok_sem, share_sem, hid_sem, y_sem, z_sem,
 ):
     rows, cols = own_ref.shape
@@ -92,13 +92,24 @@
 
     sends = []
 
-    def send(src, dst, arrived, device):
-        copy = pltpu.make_async_remote_copy(
-            src_ref=src, dst_ref=dst, send_sem=send_sem.at[len(sends)], recv_sem=arrived,
-            device_id=device, device_id_type=MESH,
-        )
-        copy.start()
-        sends.append(copy)
+    def send(make, device, allowed=None):
+        index = len(sends)
+
+        def copy():
+            src, dst, arrived = make()
+            return pltpu.make_async_remote_copy(
+                src_ref=src, dst_ref=dst, send_sem=send_sem.at[index], recv_sem=arrived,
+                device_id=device, device_id_type=MESH,
+            )
+
+        def when(action):
+            if allowed is None:
+                action()
+            else:
+                pl.when(allowed)(action)
+
+        when(lambda: copy().start())
+        sends.append(lambda: when(lambda: copy().wait_send()))
 
     def await_arrival(dst, arrived):
         pltpu.make_async_remote_copy(
@@ -111,37 +122,52 @@
             pl.ds(pl.multiple_of(s * rows, rows), rows), pl.ds(pl.multiple_of(t * cols, cols), cols)
         ]
 
-    def send_tok(s, t, device, src=None):
-        block = tok_at(s, t)
-        send(block if src is None else src, block, tok_sem.at[s, t], device)
+    def send_tok(s, t, device, src=None, allowed=None):
+        def make():
+            block = tok_at(s, t)
+            return (block if src is None else src), block, tok_sem.at[s, t]
+
+        send(make, device, allowed)
 
     def await_tok(s, t):
         await_arrival(tok_at(s, t), tok_sem.at[s, t])
 
+    upper_half = z * 2 // nz
+    mirrored = z + upper_half * (nz - 1 - 2 * z)
+
     def z_of(k):
-        return lax.rem(z - k + nz, nz)
-
-    z_peers = [(lax.rem(z + k, nz) * ny + y, part) for k in range(1, nz)]
+        near = (2 * mirrored - k + nz) // nz
+        step = -((k + 1) // 2) if k % 2 else k // 2
+        g = near * (mirrored + step) + (1 - near) * k
+        return g + upper_half * (nz - 1 - 2 * g)
+
+    def z_neighbour(z_next):
+        return (z_next * ny + y, part), (z_next >= 0) & (z_next < nz)
+
+    z_sides = [z_neighbour(z + 1), z_neighbour(z - 1)]
     send_tok(me, part, dev_x, own_ref)
     send_tok(me, part, dev_y, own_ref)
-    for peer in z_peers:
-        send_tok(me, part, peer, own_ref)
+    for device, there in z_sides:
+        send_tok(me, part, device, own_ref, there)
     send_tok(me, part, dev_sib, own_ref)
     for peer in peers[: owners - 1]:
-        send(share.at[me], share.at[me], share_sem.at[me], peer)
+        send(lambda: (share.at[me], share.at[me], share_sem.at[me]), peer)
     tok[
         pl.ds(pl.multiple_of(me * rows, rows), rows), pl.ds(pl.multiple_of(part * cols, cols), cols)
     ] = own_ref[...]
     await_tok(me, part_x)
     send_tok(me, part_x, dev_y)
-    for peer in z_peers:
-        send_tok(me, part_x, peer)
+    for device, there in z_sides:
+        send_tok(me, part_x, device, None, there)
     send_tok(me, part_x, dev_sib)
 
     def forward_z(k):
         s = z_of(k) * ny + y
+        from_below = (z - z_of(k) + nz - 1) // nz
+        device, there = z_neighbour(z - 1 + 2 * from_below)
         for t in (part, part_x):
             await_tok(s, t)
+            send_tok(s, t, device, None, there)
             send_tok(s, t, dev_y)
             send_tok(s, t, dev_sib)
 
@@ -159,27 +185,32 @@
     def group_rows(k):
         return pl.ds(pl.multiple_of(z_of(k) * group, group), group)
 
-    def hid_at(k, t):
-        return hid.at[:, group_rows(k), pl.ds(pl.multiple_of(t * units, units), units)]
-
-    nt = (((1,), (1,)), ((), ()))
+    def hid_at(k, j, t):
+        return hid.at[j, group_rows(k), pl.ds(pl.multiple_of(t * units, units), units)]
+
+    def send_hid(k, j, t, device):
+        send(lambda: (hid_at(k, j, t), hid_at(k, j, t), hid_sem.at[z_of(k), t, j]), device)
 
     def gate_up(k):
+        for i in range(splits):
+            turned[i * cols : (i + 1) * cols, :] = tok[
+                group_rows(k), i * cols : (i + 1) * cols
+            ].T
         for j in range(local_experts):
-            inputs = tok[group_rows(k), :]
-            gate = lax.dot_general(inputs, wg[j], nt, preferred_element_type=jnp.float32)
-            upper = lax.dot_general(inputs, wu[j], nt, preferred_element_type=jnp.float32)
+            gate = jnp.dot(wg[j], turned[...], preferred_element_type=jnp.float32)
+            upper = jnp.dot(wu[j], turned[...], preferred_element_type=jnp.float32)
+            mixed = gate / (1.0 + jnp.exp(-gate)) * upper
             hid[j, group_rows(k), pl.ds(pl.multiple_of(part * units, units), units)] = (
-                gate / (1.0 + jnp.exp(-gate)) * upper
-            ).astype(jnp.bfloat16)
-        for device in (dev_x, dev_sib):
-            send(hid_at(k, part), hid_at(k, part), hid_sem.at[z_of(k), part], device)
-
-    def finish_hidden(k):
-        await_arrival(hid_at(k, part_x), hid_sem.at[z_of(k), part_x])
-        send(hid_at(k, part_x), hid_at(k, part_x), hid_sem.at[z_of(k), part_x], dev_sib)
+                mixed.T.astype(jnp.bfloat16)
+            )
+            for device in (dev_x, dev_sib):
+                send_hid(k, j, part, device)
+
+    def finish_hidden(k, j):
+        await_arrival(hid_at(k, j, part_x), hid_sem.at[z_of(k), part_x, j])
+        send_hid(k, j, part_x, dev_sib)
         for t in (part_sib, part_sib_x):
-            await_arrival(hid_at(k, t), hid_sem.at[z_of(k), t])
+            await_arrival(hid_at(k, j, t), hid_sem.at[z_of(k), t, j])
 
     diagonal = lax.broadcasted_iota(jnp.int32, (rows, rows), 0) == lax.broadcasted_iota(
         jnp.int32, (rows, rows), 1
@@ -187,6 +218,7 @@
 
     def down(k):
         for j in range(local_experts):
+            finish_hidden(k, j)
             result = jnp.dot(hid[j, group_rows(k), :], wd[j], preferred_element_type=jnp.float32)
             for i in range(ny):
                 line = share[z_of(k) * ny + i, pl.ds(me * local_experts + j, 1), :]
@@ -200,7 +232,7 @@
                 else:
                     acc[k, i] += term
         ysend[k] = acc[k, other_y].astype(jnp.bfloat16)
-        send(ysend.at[k], yrecv.at[k], y_sem.at[k], dev_y)
+        send(lambda: (ysend.at[k], yrecv.at[k], y_sem.at[k]), dev_y)
 
     def reduce_y(k):
         await_arrival(yrecv.at[k], y_sem.at[k])
@@ -209,7 +241,7 @@
             acc[0, y] = total
         else:
             zsend[k] = total.astype(jnp.bfloat16)
-            send(zsend.at[k], zrecv.at[k], z_sem.at[k], (z_of(k) * ny + y, part))
+            send(lambda: (zsend.at[k], zrecv.at[z], z_sem.at[z]), (z_of(k) * ny + y, part))
 
     if nz > 1:
         forward_z(1)
@@ -228,16 +260,16 @@
             for i in range(1, owners):
                 s = lax.rem(me + i, owners)
                 await_arrival(share.at[s], share_sem.at[s])
-        finish_hidden(k)
         down(k)
     reduce_y(nz - 1)
     total = acc[0, y]
     for k in range(1, nz):
-        await_arrival(zrecv.at[k], z_sem.at[k])
-        total = total + zrecv[k].astype(jnp.float32)
+        source = lax.rem(z + k, nz)
+        await_arrival(zrecv.at[source], z_sem.at[source])
+        total = total + zrecv[source].astype(jnp.float32)
     out_ref[...] = total.astype(jnp.bfloat16)
-    for copy in sends:
-        copy.wait_send()
+    for wait in sends:
+        wait()
 
 
 def fused(owners, splits, tokens, expert_ids, gate_probs, w_gate, w_up, w_down):
@@ -249,7 +281,7 @@
     vmem = pl.BlockSpec(memory_space=pltpu.VMEM)
     hbm = pl.BlockSpec(memory_space=pl.ANY)
     dma = pltpu.SemaphoreType.DMA
-    count = 2 * (nz + 2) + (owners - 1) + 4 * (nz - 1) + 2 * nz + 3 * nz + nz + nz
+    count = 9 + (owners - 1) + 6 * (nz - 1) + 2 * nz + 3 * local_experts * nz + 2 * nz
     flops = 6 * everything * local_experts * units * width
     return pl.pallas_call(
         functools.partial(fused_kernel, owners, splits),
@@ -258,6 +290,7 @@
         out_specs=vmem,
         scratch_shapes=[
             pltpu.VMEM((everything, width), bf16),
+            pltpu.VMEM((width, PAIR * rows), bf16),
             pltpu.VMEM(w_gate.shape, bf16),
             pltpu.VMEM(w_up.shape, bf16),
             pltpu.VMEM(w_down.shape, bf16),
@@ -272,7 +305,7 @@
             dma((count,)),
             dma((owners, splits)),
             dma((owners,)),
-            dma((nz, splits)),
+            dma((nz, splits, local_experts)),
             dma((nz,)),
             dma((nz,)),
         ],
@@ -291,7 +324,7 @@
     local_experts, units, width = w_gate.shape
     everything = owners * rows
     need = 2 * (everything * width + 3 * w_gate.size + local_experts * everything * units * splits)
-    need += owners * rows * cols * 8 + 6 * rows * local_experts * width
+    need += owners * rows * cols * 8 + 4 * rows * width + 6 * rows * local_experts * width
     fits = need <= VMEM_BUDGET and rows % 128 == 0 and cols % 128 == 0 and units % 128 == 0
     if fits and splits == PAIR * PAIR and owners % PAIR == 0:
         return fused(owners, splits, tokens, expert_ids, gate_probs, w_gate, w_up, w_down)

time: 143 us -> 117 us (0.82)
  the two profiles are of different devices: /device:TPU:24 before, /device:TPU:0 now
where the time goes in v2:
time: 117 us
  Pallas kernels  115 us (98%)
  local copies, waits for them, and re-layouts  1.67 us (1%)
    pallas_call x1, Pallas kernels, fused(): pl.pallas_call(functools.partial(fused_kernel, owners, splits), out_shape...  115 us

profile of v2, /device:TPU:0, one launch (start us, length us, event | category | flops | bytes accessed | tf_op | source)
XLA Modules:
  0.0 116.5 jit_solution(400964104597689601)
XLA Ops:
  0.0 114.9 %moe.1 = bf16[128,1024]{1,0:T(8,128)(2,1)} custom-call(bf16[128,1024]{1,0:T(8,128)(2,1)} %own_ref.1, s32[8,128]{1,0:T(8,128)} %bitcast.2, f32[8,128]{1,0:T(8,128)} %bitcast.3, bf16[2,384,4096]{2,1,0:T(8,128)(2,1)} %wg_hbm.1, bf16[2,384,4096]{2,1,0:T(8,128)(2,1)} %wu_hbm.1, bf16[2,1536,1024]{2,1,0:T(8,128)(2,1)} %wd_hbm.1), custom_call_target="tpu_custom_call" | custom-call | flops 19327352832 | bytes 18874368 | tf_op jit(solution)/shard_map/moe/pallas_call | solution.py:286
  114.9 1.7 %copy.8 = bf16[128,1024]{1,0:T(8,128)(2,1)} copy(bf16[128,1024]{1,0:T(8,128)(2,1)} %moe.1) | data formatting | bytes 524288

commit v3 on v2

--- a/solution.py
+++ b/solution.py
@@ -117,20 +117,25 @@
             device_id=dev_sib, device_id_type=MESH,
         ).wait_recv()
 
-    def tok_at(s, t):
+    first = rows * 5 // 8 // 16 * 16
+    spans = ((0, first), (first, rows - first))
+
+    def tok_at(s, t, h):
+        start, size = spans[h]
         return tok.at[
-            pl.ds(pl.multiple_of(s * rows, rows), rows), pl.ds(pl.multiple_of(t * cols, cols), cols)
+            pl.ds(pl.multiple_of(s * rows + start, 16), size),
+            pl.ds(pl.multiple_of(t * cols, cols), cols),
         ]
 
-    def send_tok(s, t, device, src=None, allowed=None):
+    def send_tok(s, t, h, device, own=False, allowed=None):
         def make():
-            block = tok_at(s, t)
-            return (block if src is None else src), block, tok_sem.at[s, t]
+            block = tok_at(s, t, h)
+            return (own_ref.at[pl.ds(*spans[h]), :] if own else block), block, tok_sem.at[s, t, h]
 
         send(make, device, allowed)
 
-    def await_tok(s, t):
-        await_arrival(tok_at(s, t), tok_sem.at[s, t])
+    def await_tok(s, t, h):
+        await_arrival(tok_at(s, t, h), tok_sem.at[s, t, h])
 
     upper_half = z * 2 // nz
     mirrored = z + upper_half * (nz - 1 - 2 * z)
@@ -145,92 +150,118 @@
         return (z_next * ny + y, part), (z_next >= 0) & (z_next < nz)
 
     z_sides = [z_neighbour(z + 1), z_neighbour(z - 1)]
-    send_tok(me, part, dev_x, own_ref)
-    send_tok(me, part, dev_y, own_ref)
-    for device, there in z_sides:
-        send_tok(me, part, device, own_ref, there)
-    send_tok(me, part, dev_sib, own_ref)
+    send_tok(me, part, 0, dev_x, True)
+    for h in range(2):
+        for device, there in z_sides:
+            send_tok(me, part, h, device, True, there)
+        send_tok(me, part, h, dev_y, True)
+    send_tok(me, part, 1, dev_x, True)
+    for h in range(2):
+        send_tok(me, part, h, dev_sib, True)
     for peer in peers[: owners - 1]:
         send(lambda: (share.at[me], share.at[me], share_sem.at[me]), peer)
     tok[
         pl.ds(pl.multiple_of(me * rows, rows), rows), pl.ds(pl.multiple_of(part * cols, cols), cols)
     ] = own_ref[...]
-    await_tok(me, part_x)
-    send_tok(me, part_x, dev_y)
+    await_tok(me, part_x, 0)
     for device, there in z_sides:
-        send_tok(me, part_x, device, None, there)
-    send_tok(me, part_x, dev_sib)
+        send_tok(me, part_x, 0, device, False, there)
+    send_tok(me, part_x, 0, dev_y)
+    send_tok(me, part_x, 0, dev_sib)
 
     def forward_z(k):
         s = z_of(k) * ny + y
         from_below = (z - z_of(k) + nz - 1) // nz
         device, there = z_neighbour(z - 1 + 2 * from_below)
-        for t in (part, part_x):
-            await_tok(s, t)
-            send_tok(s, t, device, None, there)
-            send_tok(s, t, dev_y)
-            send_tok(s, t, dev_sib)
-
-    def finish_tokens(k):
-        mine, other = z_of(k) * ny + y, z_of(k) * ny + other_y
-        for t in (part, part_x):
-            await_tok(other, t)
-            send_tok(other, t, dev_sib)
-        for s in (mine, other):
-            for t in (part_sib, part_sib_x):
-                await_tok(s, t)
-
-    group = ny * rows
-
-    def group_rows(k):
-        return pl.ds(pl.multiple_of(z_of(k) * group, group), group)
-
-    def hid_at(k, j, t):
-        return hid.at[j, group_rows(k), pl.ds(pl.multiple_of(t * units, units), units)]
-
-    def send_hid(k, j, t, device):
-        send(lambda: (hid_at(k, j, t), hid_at(k, j, t), hid_sem.at[z_of(k), t, j]), device)
-
-    def gate_up(k):
+        for t, h in ((part, 0), (part, 1), (part_x, 0)):
+            await_tok(s, t, h)
+            send_tok(s, t, h, device, False, there)
+            send_tok(s, t, h, dev_y)
+            if h == 1:
+                send_tok(s, t, h, dev_x)
+            send_tok(s, t, h, dev_sib)
+
+    def relay_other(k):
+        s = z_of(k) * ny + other_y
+        for t, h in ((part, 0), (part, 1), (part_x, 0)):
+            await_tok(s, t, h)
+            if h == 1:
+                send_tok(s, t, h, dev_x)
+            send_tok(s, t, h, dev_sib)
+
+    def finish_tokens(k, side):
+        s = z_of(k) * ny + side
+        await_tok(s, part_x, 1)
+        send_tok(s, part_x, 1, dev_sib)
+        for t in (part_sib, part_sib_x):
+            for h in range(2):
+                await_tok(s, t, h)
+
+    def group_rows(k, side):
+        if side is None:
+            return pl.ds(pl.multiple_of(z_of(k) * ny * rows, rows), ny * rows)
+        return pl.ds(pl.multiple_of((z_of(k) * ny + side) * rows, rows), rows)
+
+    def hid_piece(k, side, j, t):
+        block = hid.at[
+            j, group_rows(k, side), pl.ds(pl.multiple_of(t * units, units), units)
+        ]
+        return block, hid_sem.at[z_of(k), t, j, 0 if side is None else side]
+
+    def send_hid(k, side, j, t, device):
+        def make():
+            block, arrived = hid_piece(k, side, j, t)
+            return block, block, arrived
+
+        send(make, device)
+
+    def gate_up(k, side=None):
+        size = rows if side is not None else ny * rows
         for i in range(splits):
-            turned[i * cols : (i + 1) * cols, :] = tok[
-                group_rows(k), i * cols : (i + 1) * cols
+            turned[i * cols : (i + 1) * cols, :size] = tok[
+                group_rows(k, side), i * cols : (i + 1) * cols
             ].T
         for j in range(local_experts):
-            gate = jnp.dot(wg[j], turned[...], preferred_element_type=jnp.float32)
-            upper = jnp.dot(wu[j], turned[...], preferred_element_type=jnp.float32)
+            inputs = turned[:, :size]
+            gate = jnp.dot(wg[j], inputs, preferred_element_type=jnp.float32)
+            upper = jnp.dot(wu[j], inputs, preferred_element_type=jnp.float32)
             mixed = gate / (1.0 + jnp.exp(-gate)) * upper
-            hid[j, group_rows(k), pl.ds(pl.multiple_of(part * units, units), units)] = (
+            hid[j, group_rows(k, side), pl.ds(pl.multiple_of(part * units, units), units)] = (
                 mixed.T.astype(jnp.bfloat16)
             )
             for device in (dev_x, dev_sib):
-                send_hid(k, j, part, device)
-
-    def finish_hidden(k, j):
-        await_arrival(hid_at(k, j, part_x), hid_sem.at[z_of(k), part_x, j])
-        send_hid(k, j, part_x, dev_sib)
+                send_hid(k, side, j, part, device)
+
+    def finish_hidden(k, side, j):
+        await_arrival(*hid_piece(k, side, j, part_x))
+        send_hid(k, side, j, part_x, dev_sib)
         for t in (part_sib, part_sib_x):
-            await_arrival(hid_at(k, j, t), hid_sem.at[z_of(k), t, j])
+            await_arrival(*hid_piece(k, side, j, t))
 
     diagonal = lax.broadcasted_iota(jnp.int32, (rows, rows), 0) == lax.broadcasted_iota(
         jnp.int32, (rows, rows), 1
     )
 
-    def down(k):
+    def down(k, side=None):
         for j in range(local_experts):
-            finish_hidden(k, j)
-            result = jnp.dot(hid[j, group_rows(k), :], wd[j], preferred_element_type=jnp.float32)
-            for i in range(ny):
-                line = share[z_of(k) * ny + i, pl.ds(me * local_experts + j, 1), :]
+            finish_hidden(k, side, j)
+            result = jnp.dot(
+                hid[j, group_rows(k, side), :], wd[j], preferred_element_type=jnp.float32
+            )
+            for i in range(ny if side is None else 1):
+                to = i if side is None else side
+                line = share[z_of(k) * ny + to, pl.ds(me * local_experts + j, 1), :]
                 column = jnp.sum(
                     jnp.where(diagonal, jnp.broadcast_to(line, (rows, rows)), 0.0),
                     axis=1, keepdims=True,
                 )
                 term = result[i * rows : (i + 1) * rows] * column
                 if j == 0:
-                    acc[k, i] = term
+                    acc[k, to] = term
                 else:
-                    acc[k, i] += term
+                    acc[k, to] += term
+
+    def send_y(k):
         ysend[k] = acc[k, other_y].astype(jnp.bfloat16)
         send(lambda: (ysend.at[k], yrecv.at[k], y_sem.at[k]), dev_y)
 
@@ -243,25 +274,41 @@
             zsend[k] = total.astype(jnp.bfloat16)
             send(lambda: (zsend.at[k], zrecv.at[z], z_sem.at[z]), (z_of(k) * ny + y, part))
 
-    if nz > 1:
-        forward_z(1)
-    for k in range(nz):
-        finish_tokens(k)
+    last = nz - 1
+    forward_z(1)
+    relay_other(0)
+    for k in range(last):
+        finish_tokens(k, y)
+        finish_tokens(k, other_y)
         if k == 0:
             loads[0].wait()
             loads[1].wait()
         gate_up(k)
-        if k > 0:
-            reduce_y(k - 1)
-        if k + 2 < nz:
-            forward_z(k + 2)
         if k == 0:
+            if last > 1:
+                forward_z(2)
             loads[2].wait()
             for i in range(1, owners):
                 s = lax.rem(me + i, owners)
                 await_arrival(share.at[s], share_sem.at[s])
+        else:
+            reduce_y(k - 1)
+        if k + 1 == last:
+            finish_tokens(last, y)
+            gate_up(last, y)
+        relay_other(k + 1)
         down(k)
-    reduce_y(nz - 1)
+        send_y(k)
+        if k == 0:
+            for later in range(3, nz):
+                forward_z(later)
+    finish_tokens(last, other_y)
+    gate_up(last, other_y)
+    reduce_y(last - 1)
+    down(last, y)
+    down(last, other_y)
+    send_y(last)
+    reduce_y(last)
     total = acc[0, y]
     for k in range(1, nz):
         source = lax.rem(z + k, nz)
@@ -281,7 +328,7 @@
     vmem = pl.BlockSpec(memory_space=pltpu.VMEM)
     hbm = pl.BlockSpec(memory_space=pl.ANY)
     dma = pltpu.SemaphoreType.DMA
-    count = 9 + (owners - 1) + 6 * (nz - 1) + 2 * nz + 3 * local_experts * nz + 2 * nz
+    count = 14 + (owners - 1) + 10 * (nz - 1) + 6 * nz + 3 * local_experts * (nz + 1) + 2 * nz
     flops = 6 * everything * local_experts * units * width
     return pl.pallas_call(
         functools.partial(fused_kernel, owners, splits),
@@ -303,9 +350,9 @@
             pltpu.VMEM((nz, rows, cols), bf16),
             dma((3,)),
             dma((count,)),
-            dma((owners, splits)),
+            dma((owners, splits, 2)),
             dma((owners,)),
-            dma((nz, splits, local_experts)),
+            dma((nz, splits, local_experts, PAIR)),
             dma((nz,)),
             dma((nz,)),
         ],
@@ -326,7 +373,7 @@
     need = 2 * (everything * width + 3 * w_gate.size + local_experts * everything * units * splits)
     need += owners * rows * cols * 8 + 4 * rows * width + 6 * rows * local_experts * width
     fits = need <= VMEM_BUDGET and rows % 128 == 0 and cols % 128 == 0 and units % 128 == 0
-    if fits and splits == PAIR * PAIR and owners % PAIR == 0:
+    if fits and splits == PAIR * PAIR and owners % (2 * PAIR) == 0:
         return fused(owners, splits, tokens, expert_ids, gate_probs, w_gate, w_up, w_down)
     return routed(tokens, expert_ids, gate_probs, w_gate, w_up, w_down)
 

time: 117 us -> 117 us (level)
  no operation moved by 1% of the time
where the time goes in v3:
time: 117 us
  Pallas kernels  115 us (98%)
  local copies, waits for them, and re-layouts  1.67 us (1%)
    pallas_call x1, Pallas kernels, fused(): pl.pallas_call(functools.partial(fused_kernel, owners, splits), out_shape...  115 us

profile of v3, /device:TPU:0, one launch (start us, length us, event | category | flops | bytes accessed | tf_op | source)
XLA Modules:
  0.0 116.8 jit_solution(9050634533520412260)
XLA Ops:
  0.0 115.1 %moe.1 = bf16[128,1024]{1,0:T(8,128)(2,1)} custom-call(bf16[128,1024]{1,0:T(8,128)(2,1)} %own_ref.1, s32[8,128]{1,0:T(8,128)} %bitcast.2, f32[8,128]{1,0:T(8,128)} %bitcast.3, bf16[2,384,4096]{2,1,0:T(8,128)(2,1)} %wg_hbm.1, bf16[2,384,4096]{2,1,0:T(8,128)(2,1)} %wu_hbm.1, bf16[2,1536,1024]{2,1,0:T(8,128)(2,1)} %wd_hbm.1), custom_call_target="tpu_custom_call" | custom-call | flops 19327352832 | bytes 18874368 | tf_op jit(solution)/shard_map/moe/pallas_call | solution.py:333
  115.1 1.7 %copy.8 = bf16[128,1024]{1,0:T(8,128)(2,1)} copy(bf16[128,1024]{1,0:T(8,128)(2,1)} %moe.1) | data formatting | bytes 524288

commit v4 on v3

--- a/solution.py
+++ b/solution.py
@@ -1,4 +1,5 @@
 import functools
+import math
 import jax
 import jax.numpy as jnp
 from jax import lax
@@ -8,6 +9,8 @@
 
 MESH = pl.DeviceIdType.MESH
 VMEM_BUDGET = 60 * 2**20
+CHUNK_IN = 512
+CHUNK_OUT = 256
 PAIR = 2
 
 
@@ -54,7 +57,7 @@
     owners, splits,
     own_ref, ids_ref, probs_ref, wg_hbm, wu_hbm, wd_hbm,
     out_ref,
-    tok, turned, wg, wu, wd, hid, share, acc, ysend, yrecv, zsend, zrecv,
+    tok, sums, wg, wu, wd, hid, share, acc, ysend, yrecv, zsend, zrecv,
     w_sem, send_sem, tok_sem, share_sem, hid_sem, y_sem, z_sem,
 ):
     rows, cols = own_ref.shape
@@ -215,17 +218,27 @@
 
         send(make, device)
 
+    width = tok.shape[1]
+    step_in = math.gcd(width, CHUNK_IN)
+
     def gate_up(k, side=None):
         size = rows if side is not None else ny * rows
-        for i in range(splits):
-            turned[i * cols : (i + 1) * cols, :size] = tok[
-                group_rows(k, side), i * cols : (i + 1) * cols
-            ].T
+        sums[:, :, :size] = jnp.zeros((2 * local_experts, units, size), jnp.float32)
+
+        def add(i, carry):
+            features = pl.ds(pl.multiple_of(i * step_in, step_in), step_in)
+            turned = tok[group_rows(k, side), features].T
+            for j in range(local_experts):
+                for m, w in enumerate((wg, wu)):
+                    sums[2 * j + m, :, :size] += jnp.dot(
+                        w[j, :, features], turned, preferred_element_type=jnp.float32
+                    )
+            return carry
+
+        lax.fori_loop(0, width // step_in, add, 0)
         for j in range(local_experts):
-            inputs = turned[:, :size]
-            gate = jnp.dot(wg[j], inputs, preferred_element_type=jnp.float32)
-            upper = jnp.dot(wu[j], inputs, preferred_element_type=jnp.float32)
-            mixed = gate / (1.0 + jnp.exp(-gate)) * upper
+            gate = sums[2 * j, :, :size]
+            mixed = gate / (1.0 + jnp.exp(-gate)) * sums[2 * j + 1, :, :size]
             hid[j, group_rows(k, side), pl.ds(pl.multiple_of(part * units, units), units)] = (
                 mixed.T.astype(jnp.bfloat16)
             )
@@ -242,24 +255,39 @@
         jnp.int32, (rows, rows), 1
     )
 
+    step_out = math.gcd(cols, CHUNK_OUT)
+
     def down(k, side=None):
+        places = range(ny) if side is None else (side,)
+        weights = []
         for j in range(local_experts):
             finish_hidden(k, side, j)
-            result = jnp.dot(
-                hid[j, group_rows(k, side), :], wd[j], preferred_element_type=jnp.float32
-            )
-            for i in range(ny if side is None else 1):
-                to = i if side is None else side
+            for to in places:
                 line = share[z_of(k) * ny + to, pl.ds(me * local_experts + j, 1), :]
-                column = jnp.sum(
-                    jnp.where(diagonal, jnp.broadcast_to(line, (rows, rows)), 0.0),
-                    axis=1, keepdims=True,
+                weights.append(
+                    jnp.sum(
+                        jnp.where(diagonal, jnp.broadcast_to(line, (rows, rows)), 0.0),
+                        axis=1, keepdims=True,
+                    )
                 )
-                term = result[i * rows : (i + 1) * rows] * column
-                if j == 0:
-                    acc[k, to] = term
-                else:
-                    acc[k, to] += term
+
+        def column_block(i, carry):
+            block = pl.ds(pl.multiple_of(i * step_out, step_out), step_out)
+            totals = [0.0] * len(places)
+            for j in range(local_experts):
+                result = jnp.dot(
+                    hid[j, group_rows(k, side), :], wd[j, :, block],
+                    preferred_element_type=jnp.float32,
+                )
+                for p in range(len(places)):
+                    totals[p] += (
+                        result[p * rows : (p + 1) * rows] * weights[j * len(places) + p]
+                    )
+            for p, to in enumerate(places):
+                acc[k, to, :, block] = totals[p]
+            return carry
+
+        lax.fori_loop(0, cols // step_out, column_block, 0)
 
     def send_y(k):
         ysend[k] = acc[k, other_y].astype(jnp.bfloat16)
@@ -337,7 +365,7 @@
         out_specs=vmem,
         scratch_shapes=[
             pltpu.VMEM((everything, width), bf16),
-            pltpu.VMEM((width, PAIR * rows), bf16),
+            pltpu.VMEM((2 * local_experts, units, PAIR * rows), f32),
             pltpu.VMEM(w_gate.shape, bf16),
             pltpu.VMEM(w_up.shape, bf16),
             pltpu.VMEM(w_down.shape, bf16),
@@ -371,7 +399,7 @@
     local_experts, units, width = w_gate.shape
     everything = owners * rows
     need = 2 * (everything * width + 3 * w_gate.size + local_experts * everything * units * splits)
-    need += owners * rows * cols * 8 + 4 * rows * width + 6 * rows * local_experts * width
+    need += owners * rows * cols * 8 + 16 * local_experts * units * rows + 6 * rows * local_experts * width
     fits = need <= VMEM_BUDGET and rows % 128 == 0 and cols % 128 == 0 and units % 128 == 0
     if fits and splits == PAIR * PAIR and owners % (2 * PAIR) == 0:
         return fused(owners, splits, tokens, expert_ids, gate_probs, w_gate, w_up, w_down)

time: 117 us -> 134 us (1.15)
  Pallas kernels: 115 us -> 132 us
    pallas_call x1, Pallas kernels: 115 us -> 132 us  [fused(): pl.pallas_call(functools.partial(fused_kernel, owners, splits), out_shape...]
where the time goes in v4:
time: 134 us; the launch traced here: 133 us
  Pallas kernels  132 us (99%)
  local copies, waits for them, and re-layouts  1.67 us (1%)
    pallas_call x1, Pallas kernels, fused(): pl.pallas_call(functools.partial(fused_kernel, owners, splits), out_shape...  132 us

profile of v4, /device:TPU:0, one launch (start us, length us, event | category | flops | bytes accessed | tf_op | source)
XLA Modules:
  0.0 133.4 jit_solution(10524005857571600036)
XLA Ops:
  0.0 131.8 %moe.1 = bf16[128,1024]{1,0:T(8,128)(2,1)} custom-call(bf16[128,1024]{1,0:T(8,128)(2,1)} %own_ref.1, s32[8,128]{1,0:T(8,128)} %bitcast.2, f32[8,128]{1,0:T(8,128)} %bitcast.3, bf16[2,384,4096]{2,1,0:T(8,128)(2,1)} %wg_hbm.1, bf16[2,384,4096]{2,1,0:T(8,128)(2,1)} %wu_hbm.1, bf16[2,1536,1024]{2,1,0:T(8,128)(2,1)} %wd_hbm.1), custom_call_target="tpu_custom_call" | custom-call | flops 19327352832 | bytes 18874368 | tf_op jit(solution)/shard_map/moe/pallas_call | solution.py:361
  131.8 1.7 %copy.8 = bf16[128,1024]{1,0:T(8,128)(2,1)} copy(bf16[128,1024]{1,0:T(8,128)(2,1)} %moe.1) | data formatting | bytes 524288
